TPU v7x, 256 devices: a whole 4x4x8 slice. The times are simulated.
256 devices in a mesh: expert: 16 (over x, z_lo), dp: 16 (over y, z_hi, core).
Axes of the slice: x: 4, y: 4, z: 8 (z_hi: 2, z_lo: 4; z = z_hi * 4 + z_lo), core: 2. Of those that a mesh axis runs over, the one named last changes fastest.
Arguments:
- tokens: bfloat16 [65536, 1024], P(('expert', 'dp')), may hold values from -6 to 6
- route_ids: int32 [65536, 2], P(('expert', 'dp')), may hold values from 0 to 15, all different within a row; in each aligned block of 256 rows (0 to 255, 256 to 511, ...) at most 48 rows name the same one
- gate_values: float32 [65536, 2], P(('expert', 'dp')), may hold values from 0.2 to 1
- w_gate: bfloat16 [16, 1024, 1024], P('expert', 'dp'), may hold values from -0.1875 to 0.1875
- w_up: bfloat16 [16, 1024, 1024], P('expert', 'dp'), may hold values from -0.1875 to 0.1875
- w_down: bfloat16 [16, 1024, 1024], P('expert', 'dp'), may hold values from -0.1875 to 0.1875
- swap_flags: int32 [16], replicated, may hold values from 0 to 1, as said below
- out_grad: bfloat16 [65536, 1024], P(('expert', 'dp')), may hold values from -6 to 6
Outputs:
- layer_out: bfloat16 [65536, 1024], P(('expert', 'dp'))
- grad_tokens: bfloat16 [65536, 1024], P(('expert', 'dp'))
- grad_gate: float32 [16, 1024, 1024], P('expert', 'dp')
- grad_up: float32 [16, 1024, 1024], P('expert', 'dp')
- grad_down: float32 [16, 1024, 1024], P('expert', 'dp')
Inputs may be any that keep to these rules, and one draw needn't show every extreme that they name: `route_ids`: within the rows of one device (256 tokens) no expert is named by more than 48 token-expert pairs, a bound that some block reaches; a token's 2 experts differ. `swap_flags`: the first and the last pair always exchange their experts.
All inputs are finite; a program needn't handle non-finite values.
Results may differ from a plain program's by a relative error of at most 0.012.
Values may be sent and summed in bfloat16 or wider, within the bound.
No kernel may reach another device: no remote copies, remote signals or barrier semaphores. Data moves between devices by JAX's collectives and lax.ppermute only.
A program may use at most 64 MiB of HBM per device.

v0:
```python
import jax
import jax.numpy as jnp
from jax import lax
from jax.sharding import PartitionSpec as P


def in_one_piece(arrays, axis, split_dim, concat_dim, along):
    both = jnp.concatenate(arrays, axis=along)
    whole, at, done = (
        lax.all_to_all(both, axis, split_axis=split_dim, concat_axis=concat_dim, tiled=True),
        0,
        [],
    )
    for a in arrays:
        done.append(lax.slice_in_dim(whole, at, at + a.shape[along], axis=along))
        at += a.shape[along]
    return tuple(done)


def in_one_piece_2(arrays, axis, dim, along):
    ends, at = ([], 0)
    for a in arrays[:-1]:
        at += a.shape[along]
        ends.append(at)
    both = jnp.concatenate(arrays, axis=along)
    return tuple(jnp.split(lax.all_gather(both, axis, axis=dim, tiled=True), ends, axis=along))


def sent_together(arrays, axis, dim, along):
    widths = [a.shape[along] for a in arrays]
    both = jnp.concatenate(arrays, axis=along)
    whole = lax.psum_scatter(both, axis, scatter_dimension=dim, tiled=True)
    return tuple(jnp.split(whole, [sum(widths[:k]) for k in range(1, len(widths))], axis=along))


def swapped(shard, axis, stride):
    return lax.ppermute(shard, axis, [(i, i ^ 1 << stride) for i in range(lax.axis_size(axis))])


def pair_moves(swap_flags, index_of, half_axis):
    pair_of = index_of % half_axis
    return jnp.take(swap_flags, pair_of) != jnp.take(swap_flags, pair_of + half_axis)


def route_slots(route_ids, exp_dev, axis_len, slot_cap):
    chosen = route_ids.reshape(-1)
    holder = chosen // exp_dev
    match_table = (
        chosen[:, None] == jnp.arange(exp_dev * axis_len, dtype=jnp.int32)[None, :]
    ).astype(jnp.int32)
    rank_of = jnp.sum(jnp.cumsum(match_table, axis=0) * match_table, axis=1) - 1
    return (holder * exp_dev + chosen % exp_dev) * slot_cap + rank_of


def shards(tokens, route_ids, gate_values, w_gate, w_up, w_down, swap_flags, out_grad):
    axis_len = lax.axis_size("expert")
    own_index = lax.axis_index("expert")
    half_axis = axis_len // 2
    swap_bit = axis_len.bit_length() - 2
    exp_dev = w_gate.shape[0]
    tok_rows = tokens.shape[0]
    feature_count = tokens.shape[1]
    top_k = route_ids.shape[1]
    copies = tok_rows * top_k
    slot_cap = 3 * copies // (2 * exp_dev * axis_len)
    paired_here = pair_moves(swap_flags, own_index, half_axis)
    slot_index = route_slots(route_ids, exp_dev, axis_len, slot_cap)
    total_slots = axis_len * exp_dev * slot_cap
    source = (
        jnp.full((total_slots,), copies, jnp.int32)
        .at[slot_index]
        .set(jnp.arange(copies, dtype=jnp.int32))
    )
    filled = (source < copies)[:, None]
    picked = jnp.minimum(source, copies - 1)
    weights_flat = gate_values.reshape(-1)
    buffer_shape = (axis_len, exp_dev, slot_cap, feature_count)
    send_x = jnp.where(filled, tokens[picked // top_k], jnp.zeros((), jnp.bfloat16)).reshape(
        buffer_shape
    )
    cot_rows = (
        weights_flat[picked][:, None] * out_grad[picked // top_k].astype(jnp.float32)
    ).astype(jnp.bfloat16)
    send_c = jnp.where(filled, cot_rows, jnp.zeros((), jnp.bfloat16)).reshape(buffer_shape)
    recv_x, recv_c = in_one_piece((send_x, send_c), "expert", 0, 0, 1)
    full_gate, full_up, full_down = in_one_piece_2((w_gate, w_up, w_down), "dp", 1, 0)
    pre_gate = jnp.einsum("secd,edf->secf", recv_x, full_gate, preferred_element_type=jnp.float32)
    pre_up = jnp.einsum("secd,edf->secf", recv_x, full_up, preferred_element_type=jnp.float32)
    hidden = (jax.nn.silu(pre_gate) * pre_up).astype(jnp.bfloat16)
    expert_out = jnp.einsum(
        "secf,efd->secd", hidden, full_down, preferred_element_type=jnp.float32
    ).astype(jnp.bfloat16)
    returned_out = lax.all_to_all(
        expert_out, "expert", split_axis=0, concat_axis=0, tiled=True
    ).reshape(total_slots, feature_count)
    weighted = returned_out[slot_index].astype(jnp.float32) * weights_flat[:, None]
    layer_out = jnp.sum(weighted.reshape(tok_rows, top_k, feature_count), axis=1).astype(
        jnp.bfloat16
    )
    grad_h = jnp.einsum("secd,efd->secf", recv_c, full_down, preferred_element_type=jnp.float32)
    sigmoid_a = jax.nn.sigmoid(pre_gate)
    grad_a = (grad_h * pre_up * sigmoid_a * (1.0 + pre_gate * (1.0 - sigmoid_a))).astype(
        jnp.bfloat16
    )
    grad_b = (grad_h * pre_gate * sigmoid_a).astype(jnp.bfloat16)
    copy_sum = jnp.einsum("secf,edf->secd", grad_a, full_gate, preferred_element_type=jnp.float32)
    copy_sum = copy_sum + jnp.einsum(
        "secf,edf->secd", grad_b, full_up, preferred_element_type=jnp.float32
    )
    copy_grad = copy_sum.astype(jnp.bfloat16)
    returned_grad = lax.all_to_all(
        copy_grad, "expert", split_axis=0, concat_axis=0, tiled=True
    ).reshape(total_slots, feature_count)
    grad_tokens = jnp.sum(
        returned_grad[slot_index].astype(jnp.float32).reshape(tok_rows, top_k, feature_count),
        axis=1,
    ).astype(jnp.bfloat16)
    dw_gate = jnp.einsum("secd,secf->edf", recv_x, grad_a, preferred_element_type=jnp.float32)
    dw_up = jnp.einsum("secd,secf->edf", recv_x, grad_b, preferred_element_type=jnp.float32)
    dw_down = jnp.einsum("secf,secd->efd", hidden, recv_c, preferred_element_type=jnp.float32)
    summed = tuple(
        (
            part.astype(jnp.float32)
            for part in sent_together(
                (
                    dw_gate.astype(jnp.bfloat16),
                    dw_up.astype(jnp.bfloat16),
                    dw_down.astype(jnp.bfloat16),
                ),
                "dp",
                1,
                0,
            )
        )
    )
    swapped_grads = (
        swapped(summed[0].astype(jnp.bfloat16), "expert", swap_bit).astype(jnp.float32),
        swapped(summed[1].astype(jnp.bfloat16), "expert", swap_bit).astype(jnp.float32),
        swapped(summed[2].astype(jnp.bfloat16), "expert", swap_bit).astype(jnp.float32),
    )
    summed = (
        jnp.where(paired_here, swapped_grads[0], summed[0]),
        jnp.where(paired_here, swapped_grads[1], summed[1]),
        jnp.where(paired_here, swapped_grads[2], summed[2]),
    )
    return (layer_out, grad_tokens, summed[0], summed[1], summed[2])


def solution(mesh):
    in_specs = (
        P(("expert", "dp"), None),
        P(("expert", "dp"), None),
        P(("expert", "dp"), None),
        P("expert", "dp", None),
        P("expert", "dp", None),
        P("expert", "dp", None),
        P(),
        P(("expert", "dp"), None),
    )
    out_specs = (
        P(("expert", "dp"), None),
        P(("expert", "dp"), None),
        P("expert", "dp", None),
        P("expert", "dp", None),
        P("expert", "dp", None),
    )
    return jax.shard_map(shards, mesh=mesh, in_specs=in_specs, out_specs=out_specs, check_vma=False)
```

profile of v0, /device:TPU:32, one launch (start us, length us, event | category | flops | bytes accessed | tf_op | source)
XLA Modules:
  0.0 321.4 jit_solution(628349864016758072)
XLA Ops:
  7.2 1.9 pad_maximum_fusion.2
  9.2 0.8 copy.21
  10.0 0.1 eq.29
  10.1 0.1 eq.33
  10.3 0.7 broadcast_multiply_fusion
  11.0 0.1 copy.20
  11.1 0.1 mul.72
  11.3 1.2 reduce-window.6
  12.4 0.2 slice_reduce_fusion
  12.7 0.1 fusion.35
  12.8 2.4 scatter_custom_fusion
  15.3 0.1 broadcast_in_dim.38
  15.4 2.8 gather_fusion
  18.3 3.6 %gather_fusion.2 = bf16[768,1024]{1,0:T(8,128)(2,1)} fusion(bf16[256,1024]{1,0:T(8,128)(2,1)S(1)} %copy-done.1, s32[1024]{0:T(1024)S(1)} %get-tuple-element.43), kind=kCustom, calls=%fused_computation.2 | custom fusion | bytes 3148800 | tf_op jit(solution)/shard_map/gather | solution.py:82
  21.8 0.1 copy.25
  22.0 0.1 reshape.193
  22.1 5.0 %gather_fusion.1 = f32[768]{0:T(1024)S(1)} fusion(f32[512]{0:T(512)S(1)} %reshape.193, s32[1024]{0:T(1024)S(1)} %get-tuple-element.42), kind=kCustom, calls=%fused_computation.1 | custom fusion | bytes 9216 | tf_op jit(solution)/shard_map/gather | solution.py:82
  27.2 2.2 broadcast_select_fusion
  29.4 0.3 pad_maximum_fusion.1
  29.7 112.5 %all_to_all.15 = bf16[16,2,48,1024]{3,2,1,0:T(8,128)(2,1)} all-to-all(bf16[16,2,48,1024]{3,2,1,0:T(8,128)(2,1)S(1)} %pad_maximum_fusion.1), channel_id=1, replica_groups=mesh['expert'=16,'dp'=16] {'expert'}, dimensions={0} | all-to-all | bytes 6291456 | tf_op jit(solution)/shard_map/all_to_all | solution.py:10
  142.2 4.0 %fusion.14 = f32[1024,16,48]{0,2,1:T(8,128)S(1)} fusion(bf16[3,1024,1024]{2,1,0:T(8,128)(2,1)} %all-gather.2.cloned.1.call-done, bf16[16,2,48,1024]{3,2,1,0:T(8,128)(2,1)} %all_to_all.15), kind=kOutput, calls=%fused_computation.37 | convolution fusion | flops 1610612736 | bytes 6815744 | tf_op jit(solution)/shard_map/secd,edf->secf/dot_general | solution.py:87
  146.2 0.8 copy-done.7
  147.0 1.8 fusion.16
  148.9 3.3 %fusion.5 = (bf16[16,1,48,1024]{3,2,0,1:T(8,128)(2,1)S(1)}, bf16[16,1,48,1024]{3,2,0,1:T(8,128)(2,1)S(1)}, bf16[16,1,48,1024]{3,2,0,1:T(8,128)(2,1)S(1)}) fusion(f32[1024,16,48]{0,2,1:T(8,128)S(1)} %fusion.14, f32[1024,16,48]{0,2,1:T(8,128)S(1)} %fusion.16, bf16[16,2,48,1024]{3,2,1,0:T(8,128)(2,1)S(1)} %copy-done.3, bf16[3,1024,1024]{2,1,0:T(8,128)(2,1)S(1)} %copy-done.7), kind=kOutput, calls=%fused_computation.19 | convolution fusion | flops 1623195648 | bytes 14680064 | tf_op jit(solution)/shard_map/secd,efd->secf/dot_general | solution.py:100
  152.2 1.9 fusion.20
  154.1 1.9 fusion.19
  155.9 1.9 fusion.18
  157.8 3.2 pad_maximum_fusion
  161.0 4.5 %fusion.29 = bf16[16,1,48,1024]{3,2,1,0:T(8,128)(2,1)} fusion(bf16[16,1,48,1024]{3,2,0,1:T(8,128)(2,1)S(1)} %get-tuple-element.29, bf16[3,1024,1024]{2,1,0:T(8,128)(2,1)} %all-gather.2.cloned.1.call-done), kind=kOutput, calls=%fused_computation.55 | convolution fusion | flops 1611399168 | bytes 5242880 | tf_op jit(solution)/shard_map/secf,efd->secd/dot_general | solution.py:90
  165.5 6.3 %all-to-all-start.1 = ((bf16[16,1,48,1024]{3,2,1,0:T(8,128)(2,1)}), bf16[16,1,48,1024]{3,2,1,0:T(8,128)(2,1)S(1)}, u32[]{:S(2)}, u32[]{:S(2)}) async-start(bf16[16,1,48,1024]{3,2,1,0:T(8,128)(2,1)} %fusion.29), calls=%async_computation.1 | async-start | bytes 3145728 | tf_op jit(solution)/shard_map/all_to_all | solution.py:93
  171.8 4.1 %fusion.13 = f32[1024,16,48]{0,2,1:T(8,128)S(1)} fusion(bf16[3,1024,1024]{2,1,0:T(8,128)(2,1)} %all-gather.2.cloned.1.call-done, bf16[16,1,48,1024]{3,2,0,1:T(8,128)(2,1)} %copy-done.10), kind=kOutput, calls=%fused_computation.36 | convolution fusion | flops 1610612736 | bytes 6815744 | tf_op jit(solution)/shard_map/secf,edf->secd/dot_general | solution.py:106
  175.9 4.8 %fusion.21 = bf16[16,1,48,1024]{3,2,1,0:T(8,128)(2,1)} fusion(f32[1024,16,48]{0,2,1:T(8,128)S(1)} %fusion.13, bf16[16,1,48,1024]{3,2,0,1:T(8,128)(2,1)S(1)} %copy-done.9, bf16[3,1024,1024]{2,1,0:T(8,128)(2,1)} %all-gather.2.cloned.1.call-done), kind=kOutput, calls=%fused_computation.44 | convolution fusion | flops 1612185600 | bytes 8388608 | tf_op jit(solution)/shard_map/secf,edf->secd/dot_general | solution.py:107
  180.7 55.1 %all-to-all-done.1 = bf16[16,1,48,1024]{3,2,1,0:T(8,128)(2,1)S(1)} async-done(((bf16[16,1,48,1024]{3,2,1,0:T(8,128)(2,1)}), bf16[16,1,48,1024]{3,2,1,0:T(8,128)(2,1)S(1)}, u32[]{:S(2)}, u32[]{:S(2)}) %all-to-all-start.1) | async-done | bytes 1572896 | tf_op jit(solution)/shard_map/all_to_all | solution.py:93
  235.9 1.1 copy-done.2
  237.0 10.3 %all-to-all-start.2 = ((bf16[16,1,48,1024]{3,2,1,0:T(8,128)(2,1)}), bf16[16,1,48,1024]{3,2,1,0:T(8,128)(2,1)S(1)}, u32[]{:S(2)}, u32[]{:S(2)}) async-start(bf16[16,1,48,1024]{3,2,1,0:T(8,128)(2,1)} %fusion.21), calls=%async_computation.2 | async-start | bytes 3145728 | tf_op jit(solution)/shard_map/all_to_all | solution.py:111
  247.4 0.6 fusion.42
  249.3 4.3 %gather_fusion.3 = bf16[512,1024]{1,0:T(8,128)(2,1)S(1)} fusion(bf16[768,1024]{1,0:T(8,128)(2,1)} %bitcast.166, s32[1024]{0:T(1024)S(1)} %pad_clamp_fusion), kind=kCustom, calls=%fused_computation.3 | custom fusion | bytes 2099200 | tf_op jit(solution)/shard_map/gather | solution.py:96
  253.6 2.4 reshape.245
  256.0 37.2 %reduce-scatter.2.cloned.1.call-done = bf16[3,64,1024]{2,1,0:T(8,128)(2,1)} async-done(((bf16[3,1024,1024]{2,1,0:T(8,128)(2,1)}), bf16[3,64,1024]{2,1,0:T(8,128)(2,1)}) %reduce-scatter.2.cloned.1.call-update) | async-done | bytes 393232 | tf_op jit(solution)/shard_map/reduce_scatter | solution.py:32
  293.2 1.8 fusion.41
  295.0 3.0 collective-permute-start.2
  298.0 0.6 collective-permute-start.1
  298.5 3.0 collective-permute-start
  301.5 5.1 %multiply_reduce_fusion = bf16[256,1024]{1,0:T(8,128)(2,1)} fusion(f32[256,2,1024]{2,1,0:T(2,128)} %reshape.245, f32[256,2]{1,0:T(8,128)S(1)} %copy.25), kind=kLoop, calls=%fused_computation.33 | loop fusion | flops 786432 | bytes 2623488 | tf_op jit(solution)/shard_map/reduce_sum | solution.py:97
  306.7 2.1 gather_fusion.4
  308.7 0.4 gather.32
  309.2 3.6 %reduce_sum.32 = bf16[256,1024]{1,0:T(8,128)(2,1)} reduce(bf16[256,2,1024]{2,1,0:T(2,128)(2,1)S(1)} %gather.32, bf16[]{:T(256)} %constant.95.clone.1), dimensions={1}, to_apply=%region_5.6 | reduce | flops 262144 | bytes 1572866 | tf_op jit(solution)/shard_map/reduce_sum | solution.py:114
  312.8 1.8 convert_select_fusion
  (40 shorter events, 0.3 us)
Async XLA Ops:
  7.2 8.2 %copy-start = (bf16[256,1024]{1,0:T(8,128)(2,1)S(1)}, bf16[256,1024]{1,0:T(8,128)(2,1)}, u32[]{:S(2)}) copy-start(bf16[256,1024]{1,0:T(8,128)(2,1)} %param.8) | copy-start | bytes 1572868
  7.2 135.0 %all-gather.2.cloned.1.call-start = ((), (), s32[]{:S(2)}) async-start(), calls=%async_computation.4 | async-start | bytes 6684672 | tf_op jit(solution)/shard_map/all_gather | solution.py:26
  9.1 284.1 %reduce-scatter.2.cloned.1.call-start = ((), (), s32[]{:S(2)}) async-start(), calls=%async_computation.5 | async-start | bytes 6684672 | tf_op jit(solution)/shard_map/reduce_scatter | solution.py:32
  15.4 2.8 copy-start.1
  18.3 3.6 %copy-start.5 = (f32[256,2]{0,1:T(2,128)S(1)}, f32[256,2]{0,1:T(2,128)}, u32[]{:S(2)}) copy-start(f32[256,2]{0,1:T(2,128)} %param.10) | copy-start | bytes 6148
  142.2 4.0 %copy-start.3 = (bf16[16,2,48,1024]{3,2,1,0:T(8,128)(2,1)S(1)}, bf16[16,2,48,1024]{3,2,1,0:T(8,128)(2,1)}, u32[]{:S(2)}) copy-start(bf16[16,2,48,1024]{3,2,1,0:T(8,128)(2,1)} %all_to_all.15) | copy-start | bytes 9437188
  142.2 4.8 %copy-start.7 = (bf16[3,1024,1024]{2,1,0:T(8,128)(2,1)S(1)}, bf16[3,1024,1024]{2,1,0:T(8,128)(2,1)}, u32[]{:S(2)}) copy-start(bf16[3,1024,1024]{2,1,0:T(8,128)(2,1)} %all-gather.2.cloned.1.call-done) | copy-start | bytes 18874372
  152.2 1.9 copy-start.8
  152.2 3.8 %copy-start.10 = (bf16[16,1,48,1024]{3,2,0,1:T(8,128)(2,1)}, bf16[16,1,48,1024]{3,2,0,1:T(8,128)(2,1)S(1)}, u32[]{:S(2)}) copy-start(bf16[16,1,48,1024]{3,2,0,1:T(8,128)(2,1)S(1)} %get-tuple-element.28) | copy-start | bytes 4718596
  165.5 70.3 %all-to-all-start.1 = ((bf16[16,1,48,1024]{3,2,1,0:T(8,128)(2,1)}), bf16[16,1,48,1024]{3,2,1,0:T(8,128)(2,1)S(1)}, u32[]{:S(2)}, u32[]{:S(2)}) async-start(bf16[16,1,48,1024]{3,2,1,0:T(8,128)(2,1)} %fusion.29), calls=%async_computation.1 | async-start | bytes 3145728 | tf_op jit(solution)/shard_map/all_to_all | solution.py:93
  171.8 4.1 %copy-start.9 = (bf16[16,1,48,1024]{3,2,0,1:T(8,128)(2,1)S(1)}, bf16[16,1,48,1024]{3,2,0,1:T(8,128)(2,1)}, u32[]{:S(2)}) copy-start(bf16[16,1,48,1024]{3,2,0,1:T(8,128)(2,1)} %copy-done.8) | copy-start | bytes 4718596
  180.7 66.6 %copy-start.6 = (s32[16]{0:T(128)S(1)}, s32[16]{0:T(128)}, u32[]{:S(2)}) copy-start(s32[16]{0:T(128)} %param.14) | copy-start | bytes 196
  235.9 1.1 copy-start.2
  237.0 69.6 %all-to-all-start.2 = ((bf16[16,1,48,1024]{3,2,1,0:T(8,128)(2,1)}), bf16[16,1,48,1024]{3,2,1,0:T(8,128)(2,1)S(1)}, u32[]{:S(2)}, u32[]{:S(2)}) async-start(bf16[16,1,48,1024]{3,2,1,0:T(8,128)(2,1)} %fusion.21), calls=%async_computation.2 | async-start | bytes 3145728 | tf_op jit(solution)/shard_map/all_to_all | solution.py:111
  295.0 17.7 %collective-permute-start.2 = (bf16[1,64,1024]{2,1,0:T(8,128)(2,1)}, bf16[1,64,1024]{2,1,0:T(8,128)(2,1)S(1)}, u32[]{:S(2)}, u32[]{:S(2)}) collective-permute-start(bf16[1,64,1024]{2,1,0:T(8,128)(2,1)} %get-tuple-element.33), channel_id=1, source_target_pairs={{0,128},{16,144},{32,160},{48,176},{64,192},{80,208},{96,224},{112... | collective-permute-start | bytes 393224 | tf_op jit(solution)/shard_map/ppermute | solution.py:37
  298.0 14.8 %collective-permute-start.1 = (bf16[1,64,1024]{2,1,0:T(8,128)(2,1)}, bf16[1,64,1024]{2,1,0:T(8,128)(2,1)S(1)}, u32[]{:S(2)}, u32[]{:S(2)}) collective-permute-start(bf16[1,64,1024]{2,1,0:T(8,128)(2,1)} %get-tuple-element.34), channel_id=1, source_target_pairs={{0,128},{16,144},{32,160},{48,176},{64,192},{80,208},{96,224},{112... | collective-permute-start | bytes 393224 | tf_op jit(solution)/shard_map/ppermute | solution.py:37
  298.5 14.2 %collective-permute-start = (bf16[1,64,1024]{2,1,0:T(8,128)(2,1)}, bf16[1,64,1024]{2,1,0:T(8,128)(2,1)}, u32[]{:S(2)}, u32[]{:S(2)}) collective-permute-start(bf16[1,64,1024]{2,1,0:T(8,128)(2,1)} %get-tuple-element.35), channel_id=1, source_target_pairs={{0,128},{16,144},{32,160},{48,176},{64,192},{80,208},{96,224},{112... | collective-permute-start | bytes 393224 | tf_op jit(solution)/shard_map/ppermute | solution.py:37
  308.7 4.1 %copy-start.4 = (bf16[3,64,1024]{2,1,0:T(8,128)(2,1)S(1)}, bf16[3,64,1024]{2,1,0:T(8,128)(2,1)}, u32[]{:S(2)}) copy-start(bf16[3,64,1024]{2,1,0:T(8,128)(2,1)} %reduce-scatter.2.cloned.1.call-done) | copy-start | bytes 1179652
Sparse Core Ops, SparseCore 0:
  11.3 111.0 all-gather.1
  161.1 132.0 reduce-scatter.1
where the time goes:
time: 322 us; the launch traced here: 321 us
  blocking collectives  112 us (35%)
  waiting for transfers between devices  92.4 us (29%)
  local copies, waits for them, and re-layouts  29.4 us (9%)
  matrix products  28.2 us (9%)
  starting transfers between devices  23.2 us (7%)
  other arithmetic  20.1 us (6%)
  between operations  15.7 us (5%)
    all_to_all x1, blocking collectives, in_one_piece(): lax.all_to_all(both, axis, split_axis=split_dim, concat_axis=concat_dim,...  112 us
    all_to_all x1, waiting for transfers between devices, shards(): lax.all_to_all(expert_out, 'expert', split_axis=0, concat_axis=0, tiled=T...  55.1 us
    reduce_scatter x1, waiting for transfers between devices, sent_together(): whole = lax.psum_scatter(both, axis, scatter_dimension=dim, tiled=True)  37.2 us
    all_to_all x1, starting transfers between devices, shards(): lax.all_to_all(copy_grad, 'expert', split_axis=0, concat_axis=0, tiled=True)  10.3 us
    ppermute x3, starting transfers between devices, swapped(): lax.ppermute(shard, axis, [(i, i ^ 1 << stride) for i in range(lax.axis_s...  6.5 us
  transfers between devices with their start and end apart: 7, of which 2 were waited for; matrix products, arithmetic and copies ran while one was open for 17% of the time, Pallas kernels for 0%

commit v1 on v0

v1 whole, which is shorter than its diff:
```python
import jax
import jax.numpy as jnp
from jax import lax
from jax.experimental import pallas as pl
from jax.experimental.pallas import tpu as pltpu
from jax.sharding import Mesh, PartitionSpec as P

AXES = ("x", "z_lo", "y", "z_hi", "core")
SIZES = (4, 4, 4, 2, 2)
CAP = 48
BF16 = jnp.bfloat16
F32 = jnp.float32
VMEM = pl.BlockSpec(memory_space=pltpu.VMEM)
SMEM = pl.BlockSpec(memory_space=pltpu.SMEM)


def flat(x, zl, y, zh, c):
    return (((x * 4 + zl) * 4 + y) * 2 + zh) * 2 + c


def z_pairs(j, back):
    pairs = []
    for x in range(4):
        for zl in range(4):
            for y in range(4):
                for zh in range(2):
                    for c in range(2):
                        step = (0, 1, 2 if c == 0 else -2, -1)[j]
                        z = (zh * 4 + zl + step) % 8
                        here, there = flat(x, zl, y, zh, c), flat(x, z % 4, y, z // 4, c)
                        pairs.append((there, here) if back else (here, there))
    return pairs


def z_move(a, j, back=False):
    return a if j == 0 else lax.ppermute(a, AXES, z_pairs(j, back))


def y_move(a, step):
    return lax.ppermute(a, "y", [(i, (i + step) % 4) for i in range(4)])


def x_swap(a):
    return lax.ppermute(a, "x", [(i, i ^ 2) for i in range(4)])


def x_exchange(a):
    return lax.all_to_all(a, "x", split_axis=0, concat_axis=0, tiled=True)


def flip(a, axis):
    return lax.ppermute(a, axis, [(0, 1), (1, 0)])


def iota(shape, dim):
    return lax.broadcasted_iota(jnp.int32, shape, dim)


def shape(*dims, dtype=BF16):
    return jax.ShapeDtypeStruct(dims, dtype)


def call(body, outs, ins, scratch=(), vmem=24, flops=0, moved=2**20):
    return pl.pallas_call(
        body,
        out_shape=outs,
        in_specs=ins,
        scratch_shapes=scratch,
        compiler_params=pltpu.CompilerParams(vmem_limit_bytes=vmem * 2**20),
        cost_estimate=pl.CostEstimate(flops=flops, bytes_accessed=moved, transcendentals=0),
    )


def copies(arrays, outs, pieces):
    n = len(arrays)

    def body(*refs):
        for i, at, o, to in pieces:
            refs[n + o][to] = refs[i][at]

    return pl.pallas_call(
        body,
        out_shape=tuple(outs),
        in_specs=[VMEM] * n,
        out_specs=tuple(VMEM for _ in outs),
        compiler_params=pltpu.CompilerParams(vmem_limit_bytes=16 * 2**20),
        cost_estimate=pl.CostEstimate(flops=0, bytes_accessed=4 * 2**20, transcendentals=0),
    )(*arrays)


ALL = slice(None)


def stack(arrays):
    return copies(
        arrays, [shape(len(arrays), *arrays[0].shape)], [(i, ALL, 0, i) for i in range(len(arrays))]
    )[0]


def join_classes(arrays):
    d = arrays[0].shape[-1]
    return copies(arrays, [shape(4, 4, CAP, d)], [(j, ALL, 0, (ALL, j)) for j in range(4)])[0]


def split_classes(a):
    d = a.shape[-1]
    return copies((a,), [shape(4, CAP, d)] * 4, [(0, (ALL, j), j, ALL) for j in range(4)])


def prep_kernel(place, flags, ids_ref, gate_ref, tok_ref, grad_ref, x0, x1, x2, x3, c_ref, slot_ref):
    t = ids_ref.shape[0]
    zl = place[3]
    ids = ids_ref[...]
    shift = jnp.zeros_like(ids)
    for p in range(8):
        step = jnp.where(flags[p] != flags[p + 8], 8, 0)
        shift = shift + jnp.where((ids & 7) == p, step, 0)
    holder = (ids + shift) & 15
    hx, hj = holder >> 2, ((holder & 3) - zl) & 3
    lab = hj * 4 + hx
    hot = [lab[:, k : k + 1] == iota((t, 16), 1) for k in range(2)]
    both = jnp.where(hot[0] | hot[1], 1.0, 0.0).astype(BF16)
    earlier = jnp.where(iota((t, t), 1) < iota((t, t), 0), 1.0, 0.0).astype(BF16)
    count = jnp.dot(earlier, both, preferred_element_type=F32)
    diagonal = iota((t, t), 0) == iota((t, t), 1)
    gate = gate_ref[...]
    slot, weight = [], []
    for k in range(2):
        rank = jnp.sum(jnp.where(hot[k], count, 0.0), axis=1, keepdims=True).astype(jnp.int32)
        col = lab[:, k : k + 1] * CAP + rank
        slot_ref[:, k : k + 1] = col
        slot_ref[:, k + 2 : k + 3] = (hx[:, k : k + 1] * 4 + hj[:, k : k + 1]) * CAP + rank
        slot.append(
            jnp.sum(jnp.where(diagonal, col.astype(F32), 0.0), axis=0, keepdims=True).astype(jnp.int32)
        )
        weight.append(jnp.sum(jnp.where(diagonal, gate[:, k : k + 1], 0.0), axis=0, keepdims=True))
    tok = tok_ref[...]
    grad = grad_ref[...]
    for j, out in enumerate((x0, x1, x2, x3)):
        rows = iota((4 * CAP, t), 0) + j * 4 * CAP
        m0, m1 = rows == slot[0], rows == slot[1]
        pick = jnp.where(m0 | m1, 1.0, 0.0).astype(BF16)
        scale = jnp.sum(
            jnp.where(m0, weight[0], 0.0) + jnp.where(m1, weight[1], 0.0), axis=1, keepdims=True
        )
        xr = jnp.dot(pick, tok, preferred_element_type=F32).astype(BF16)
        cr = (scale * jnp.dot(pick, grad, preferred_element_type=F32)).astype(BF16)
        for e in range(4):
            out[e] = xr[e * CAP : (e + 1) * CAP]
            c_ref[e, j] = cr[e * CAP : (e + 1) * CAP]


def mix_kernel(slot_ref, gate_ref, rows_ref, out_ref):
    gate = gate_ref[...]
    t, s = gate.shape[0], rows_ref.shape[0]
    rows = rows_ref[...]
    total = None
    for k in range(2):
        pick = jnp.where(iota((t, s), 1) == slot_ref[:, k + 2 : k + 3], 1.0, 0.0).astype(BF16)
        part = gate[:, k : k + 1] * jnp.dot(pick, rows, preferred_element_type=F32)
        total = part if total is None else total + part
    out_ref[...] = total.astype(BF16)


def add_kernel(slot_ref, r0, r1, r2, r3, out_ref):
    t = slot_ref.shape[0]
    total = None
    for j, ref in enumerate((r0, r1, r2, r3)):
        at = iota((t, 4 * CAP), 1) + j * 4 * CAP
        pick = jnp.where((at == slot_ref[:, 0:1]) | (at == slot_ref[:, 1:2]), 1.0, 0.0).astype(BF16)
        part = jnp.dot(pick, ref[...], preferred_element_type=F32)
        total = part if total is None else total + part
    out_ref[...] = total.astype(BF16)


def dot(a, b, ca, cb):
    return lax.dot_general(a, b, (((ca,), (cb,)), ((), ())), preferred_element_type=F32)


def expert_kernel(place, x_ref, c0, c1, c2, c3, near, near2, far, far2,
                  o0, o1, o2, o3, cg, mine, other, w, xs, cs, hid, ga, gb):
    y, zh, core = place[0], place[1], place[2]
    d = xs.shape[1]
    for m in range(3):
        for side, (n, f) in enumerate(((near, far), (near2, far2))):
            c = lax.rem(core + side, 2)
            for k, step in enumerate((0, 3, 1)):
                for h in range(2):
                    at = ((lax.rem(y + step, 4) * 2 + lax.rem(zh + h, 2)) * 2 + c) * 64
                    w[m, pl.ds(pl.multiple_of(at, 64), 64), :] = n[2 * k + h, m]
            for h in range(2):
                at = ((lax.rem(y + 2, 4) * 2 + lax.rem(zh + h, 2)) * 2 + c) * 64
                for q in range(2):
                    to = pl.multiple_of(at + 32 * q, 32)
                    w[m, pl.ds(to, 32), :] = f[q, m, 32 * h : 32 * h + 32]
    for j, c in enumerate((c0, c1, c2, c3)):
        for s in range(4):
            at = (j * 4 + s) * CAP
            xs[at : at + CAP] = x_ref[s, j]
            cs[at : at + CAP] = c[s]

    def first(n, _):
        cols = pl.ds(pl.multiple_of(n * 256, 256), 256)
        for r in range(3):
            rows = slice(r * 256, r * 256 + 256)
            pre_gate = dot(xs[rows], w[0, :, cols], 1, 0)
            pre_up = dot(xs[rows], w[1, :, cols], 1, 0)
            grad_h = dot(cs[rows], w[2, cols, :], 1, 1)
            sig = jax.nn.sigmoid(pre_gate)
            act = pre_gate * sig
            hid[rows, cols] = (act * pre_up).astype(BF16)
            ga[rows, cols] = (grad_h * pre_up * sig * (1.0 + pre_gate * (1.0 - sig))).astype(BF16)
            gb[rows, cols] = (grad_h * act).astype(BF16)
        return 0

    lax.fori_loop(0, 4, first, 0)

    def weight_grads(n, _):
        cols = pl.ds(pl.multiple_of(n * 256, 256), 256)
        rel = lax.rem(n + 4 - y, 4)
        for m, (left, right) in enumerate(((xs, ga), (xs, gb), (hid, cs))):
            part = dot(left[:, cols], right[...], 0, 0).astype(BF16)
            for h in range(2):
                p0, p1 = part[h * 128 : h * 128 + 64], part[h * 128 + 64 : h * 128 + 128]
                mine[rel, m, h] = jnp.where(core == 0, p0, p1)
                other[rel, m, h] = jnp.where(core == 0, p1, p0)
        return 0

    lax.fori_loop(0, 4, weight_grads, 0)

    def returns(n, _):
        cols = pl.ds(pl.multiple_of(n * 256, 256), 256)
        for j, o in enumerate((o0, o1, o2, o3)):
            rows = slice(j * 4 * CAP, (j + 1) * 4 * CAP)
            out = dot(hid[rows], w[2, :, cols], 1, 0).astype(BF16)
            back = (dot(ga[rows], w[0, cols, :], 1, 1) + dot(gb[rows], w[1, cols, :], 1, 1)).astype(BF16)
            for s in range(4):
                o[s, :, cols] = out[s * CAP : (s + 1) * CAP]
                cg[s, j, :, cols] = back[s * CAP : (s + 1) * CAP]
        return 0

    lax.fori_loop(0, 4, returns, 0)


def plus(a, b):
    return a.astype(F32) + b.astype(F32)


def far_kernel(mine, came, to_r, to_l):
    to_r[...] = plus(mine[2, :, :, 0:32], came[2, :, :, 0:32]).astype(BF16)
    to_l[...] = plus(mine[2, :, :, 32:64], came[2, :, :, 32:64]).astype(BF16)


def side_kernel(mine, came, fr, fl, to_r, to_l):
    lo, hi = slice(0, 32), slice(32, 64)
    to_r[:, :, lo] = (plus(mine[1, :, :, lo], came[1, :, :, lo]) + fr[...].astype(F32)).astype(BF16)
    to_r[:, :, hi] = plus(mine[1, :, :, hi], came[1, :, :, hi]).astype(BF16)
    to_l[:, :, lo] = plus(mine[3, :, :, lo], came[3, :, :, lo]).astype(BF16)
    to_l[:, :, hi] = (plus(mine[3, :, :, hi], came[3, :, :, hi]) + fl[...].astype(F32)).astype(BF16)


def here_kernel(place, mine, came, fr, fl, away, here):
    zh = place[1]
    for z, out in ((zh, here), (1 - zh, away)):
        total = plus(mine[0, :, z], came[0, :, z]) + plus(fr[:, z], fl[:, z])
        out[...] = total.astype(out.dtype)


def last_kernel(here, came, a, b, c):
    for m, out in enumerate((a, b, c)):
        out[0] = here[m] + came[m].astype(F32)


def shards(tokens, route_ids, gate_values, w_gate, w_up, w_down, swap_flags, out_grad):
    xi, zl = lax.axis_index("x"), lax.axis_index("z_lo")
    yi, zh, core = lax.axis_index("y"), lax.axis_index("z_hi"), lax.axis_index("core")
    t, d = tokens.shape
    own = xi * 4 + zl
    moved = swap_flags[own % 8] != swap_flags[own % 8 + 8]
    place = jnp.stack([yi, zh, core, zl]).astype(jnp.int32)
    flags = swap_flags.astype(jnp.int32)
    piece = shape(4, CAP, d)

    w_own = stack((w_gate[0], w_up[0], w_down[0]))
    w = jnp.where(moved, x_swap(w_own), w_own)
    *sent_x, sent_c, slot = call(
        prep_kernel,
        (piece, piece, piece, piece, shape(4, 4, CAP, d), shape(t, 4, dtype=jnp.int32)),
        [SMEM, SMEM] + [VMEM] * 4,
        flops=4 * 16 * CAP * t * d,
        moved=4 * 2**20,
    )(place, flags, route_ids, gate_values, tokens, out_grad)
    w, sent_x, sent_c = lax.optimization_barrier((w, sent_x, sent_c))
    w2 = flip(w, "z_hi")
    r0, l0 = y_move(w, 1), y_move(w, 3)

    came_x = [z_move(sent_x[j], j) for j in range(4)]
    came_c = x_exchange(sent_c)
    w2, came_x = lax.optimization_barrier((w2, came_x))
    r1, l1 = y_move(w2, 1), y_move(w2, 3)

    recv_x = x_exchange(join_classes(came_x))
    recv_c = [z_move(a, j) for j, a in enumerate(split_classes(came_c))]
    half = shape(3, 64, d)
    lo, hi = (ALL, slice(0, 32)), (ALL, slice(32, 64))
    near, to_r, to_l = copies(
        (w, w2, r0, r1, l0, l1),
        [shape(6, 3, 64, d), half, half],
        [(i, ALL, 0, i) for i in range(6)] + [(2, lo, 1, lo), (3, lo, 1, hi), (4, hi, 2, lo), (5, hi, 2, hi)],
    )
    fr, fl = y_move(to_r, 1), y_move(to_l, 3)
    near2 = flip(near, "core")
    far = stack((fr, fl))
    far2 = flip(far, "core")

    bf = lambda *dims: pltpu.VMEM(dims, BF16)
    *out, copy_grad, mine, other = call(
        expert_kernel,
        (piece, piece, piece, piece, shape(4, 4, CAP, d), shape(4, 3, 2, 64, d), shape(4, 3, 2, 64, d)),
        [SMEM] + [VMEM] * 9,
        [bf(3, d, d)] + [bf(16 * CAP, d) for _ in range(5)],
        vmem=52,
        flops=18 * 16 * CAP * d * d,
        moved=20 * 2**20,
    )(place, recv_x, *recv_c, near, near2, far, far2)

    out = [z_move(out[j], j, True) for j in range(4)]
    ret = x_exchange(copy_grad)
    came = flip(other, "core")
    piece3, row3 = shape(3, 2, 64, d), shape(3, 2, 32, d)
    to_r, to_l = call(far_kernel, (row3, row3), [VMEM] * 2)(mine, came)
    fr, fl = y_move(to_r, 1), y_move(to_l, 3)
    fr, fl, out = lax.optimization_barrier((fr, fl, out))
    to_r, to_l = call(side_kernel, (piece3, piece3), [VMEM] * 4)(mine, came, fr, fl)
    fr, fl = y_move(to_r, 1), y_move(to_l, 3)
    ret = [z_move(a, j, True).reshape(-1, d) for j, a in enumerate(split_classes(ret))]
    back = x_exchange(join_classes(out)).reshape(-1, d)
    fr, fl, ret = lax.optimization_barrier((fr, fl, ret))
    away, here = call(here_kernel, (shape(3, 64, d), shape(3, 64, d, dtype=F32)), [SMEM] + [VMEM] * 4)(
        place, mine, came, fr, fl
    )
    came = flip(away, "z_hi")
    layer_out = call(
        mix_kernel, shape(t, d), [VMEM] * 3, flops=4 * 16 * CAP * t * d, moved=2 * 2**20
    )(slot, gate_values, back)
    grad_tokens = call(
        add_kernel, shape(t, d), [VMEM] * 5, flops=2 * 16 * CAP * t * d, moved=2 * 2**20
    )(slot, *ret)
    one = shape(1, 64, d, dtype=F32)
    grads = call(last_kernel, (one, one, one), [VMEM] * 2)(here, came)
    return layer_out, grad_tokens, *grads


def solution(mesh):
    fine = Mesh(mesh.devices.reshape(SIZES), AXES)
    rows = P(AXES, None)
    weight = P(("x", "z_lo"), ("y", "z_hi", "core"), None)
    return jax.shard_map(
        shards,
        mesh=fine,
        in_specs=(rows, rows, rows, weight, weight, weight, P(), rows),
        out_specs=(rows, rows, weight, weight, weight),
        check_vma=False,
    )
```

time: 322 us -> 231 us (0.72)
  the two profiles are of different devices: /device:TPU:32 before, /device:TPU:99 now
where the time goes in v1:
time: 231 us; the launch traced here: 230 us
  waiting for transfers between devices  109 us (47%)
  starting transfers between devices  53.8 us (23%)
  Pallas kernels  48.8 us (21%)
  local copies, waits for them, and re-layouts  16.3 us (7%)
    ppermute x12, waiting for transfers between devices, z_move(): return a if j == 0 else lax.ppermute(a, AXES, z_pairs(j, back))  64.8 us
    ppermute x5, waiting for transfers between devices, flip(): return lax.ppermute(a, axis, [(0, 1), (1, 0)])  33.4 us
    pallas_call x1, Pallas kernels, shards(): call(expert_kernel, (piece, piece, piece, piece, shape(4, 4, CAP, d), sha...  25.5 us
    all_to_all x4, starting transfers between devices, x_exchange(): return lax.all_to_all(a, 'x', split_axis=0, concat_axis=0, tiled=True)  20.4 us
    ppermute x10, starting transfers between devices, y_move(): return lax.ppermute(a, 'y', [(i, (i + step) % 4) for i in range(4)])  15.1 us
    unnamed x54, local copies, waits for them, and re-layouts  14.9 us
    ppermute x12, starting transfers between devices, z_move(): return a if j == 0 else lax.ppermute(a, AXES, z_pairs(j, back))  10.7 us
    pallas_call x7, Pallas kernels, copies(): pl.pallas_call(body, out_shape=tuple(outs), in_specs=[VMEM] * n, out_spec...  6.3 us
  transfers between devices with their start and end apart: 32, of which 17 were waited for; matrix products, arithmetic and copies ran while one was open for 1% of the time, Pallas kernels for 10%

profile of v1, /device:TPU:99, one launch (start us, length us, event | category | flops | bytes accessed | tf_op | source)
XLA Modules:
  0.0 230.1 jit_solution(6216705338370770153)
XLA Ops:
  3.4 1.9 collective-permute-start
  7.0 1.4 fusion
  10.4 1.0 copy-done.17
  11.4 1.0 copy-done.18
  12.4 3.5 %shard_map.119 = (bf16[4,48,1024]{2,1,0:T(8,128)(2,1)S(1)}, bf16[4,48,1024]{2,1,0:T(8,128)(2,1)S(1)}, bf16[4,48,1024]{2,1,0:T(8,128)(2,1)S(1)}, bf16[4,48,1024]{...) custom-call(s32[4]{0:T(128)S(1)} %pad_add_fusion.place, s32[16]{0:T(128)S(1)} %copy-done.16, ...), custom_call_target="tpu_custom_call" | custom-call | flops 805306368 | bytes 4194304 | tf_op jit(solution)/shard_map/pallas_call | solution.py:286
  16.0 2.9 %collective-permute-start.2 = (bf16[4,48,1024]{2,1,0:T(8,128)(2,1)S(1)}, bf16[4,48,1024]{2,1,0:T(8,128)(2,1)S(1)}, u32[]{:S(2)}, u32[]{:S(2)}) collective-permute-start(bf16[4,48,1024]{2,1,0:T(8,128)(2,1)S(1)} %get-tuple-element.69), channel_id=1, source_target_pairs={{0,16},{1,17},{2,18},{3,19},{4,20},{5,21},{6,22},{7,23},{8,24},{9,... | collective-permute-start | bytes 1179656 | tf_op jit(solution)/shard_map/ppermute | solution.py:36
  18.9 4.0 %collective-permute-start.1 = (bf16[3,64,1024]{2,1,0:T(8,128)(2,1)S(1)}, bf16[3,64,1024]{2,1,0:T(8,128)(2,1)}, u32[]{:S(2)}, u32[]{:S(2)}) collective-permute-start(bf16[3,64,1024]{2,1,0:T(8,128)(2,1)S(1)} %broadcast_select_fusion.refs_0_), channel_id=1, source_target_pairs={{0,2},{2,0},{1,3},{3,1},{4,6},{6,4},{5,7},{7,5},{8,10},{10,8},{9,1... | collective-permute-start | bytes 1179656 | tf_op jit(solution)/shard_map/ppermute | solution.py:52
  22.9 2.7 %collective-permute-start.10 = (bf16[3,64,1024]{2,1,0:T(8,128)(2,1)S(1)}, bf16[3,64,1024]{2,1,0:T(8,128)(2,1)}, u32[]{:S(2)}, u32[]{:S(2)}) collective-permute-start(bf16[3,64,1024]{2,1,0:T(8,128)(2,1)S(1)} %broadcast_select_fusion.refs_0_), channel_id=1, source_target_pairs={{0,12},{4,0},{8,4},{12,8},{1,13},{5,1},{9,5},{13,9},{2,14},{6,2},{... | collective-permute-start | bytes 1179656 | tf_op jit(solution)/shard_map/ppermute | solution.py:40
  25.6 3.5 %collective-permute-done.2.refs_1_ = bf16[4,48,1024]{2,1,0:T(8,128)(2,1)S(1)} collective-permute-done((bf16[4,48,1024]{2,1,0:T(8,128)(2,1)S(1)}, bf16[4,48,1024]{2,1,0:T(8,128)(2,1)S(1)}, u32[]{:S(2)}, u32[]{:S(2)}) %collective-permute-start.2) | collective-permute-done | bytes 393248 | tf_op jit(solution)/shard_map/ppermute | solution.py:36
  29.1 1.3 collective-permute-start.8
  30.4 3.2 %collective-permute-done.3.refs_2_ = bf16[4,48,1024]{2,1,0:T(8,128)(2,1)S(1)} collective-permute-done((bf16[4,48,1024]{2,1,0:T(8,128)(2,1)S(1)}, bf16[4,48,1024]{2,1,0:T(8,128)(2,1)S(1)}, u32[]{:S(2)}, u32[]{:S(2)}) %collective-permute-start.3) | collective-permute-done | bytes 393248 | tf_op jit(solution)/shard_map/ppermute | solution.py:36
  33.6 6.9 %collective-permute-done.4.refs_3_ = bf16[4,48,1024]{2,1,0:T(8,128)(2,1)S(1)} collective-permute-done((bf16[4,48,1024]{2,1,0:T(8,128)(2,1)S(1)}, bf16[4,48,1024]{2,1,0:T(8,128)(2,1)S(1)}, u32[]{:S(2)}, u32[]{:S(2)}) %collective-permute-start.4) | collective-permute-done | bytes 393248 | tf_op jit(solution)/shard_map/ppermute | solution.py:36
  40.6 16.4 %collective-permute-done.1.refs_1_ = bf16[3,64,1024]{2,1,0:T(8,128)(2,1)} collective-permute-done((bf16[3,64,1024]{2,1,0:T(8,128)(2,1)S(1)}, bf16[3,64,1024]{2,1,0:T(8,128)(2,1)}, u32[]{:S(2)}, u32[]{:S(2)}) %collective-permute-start.1) | collective-permute-done | bytes 393248 | tf_op jit(solution)/shard_map/ppermute | solution.py:52
  57.0 2.7 %collective-permute-start.11 = (bf16[3,64,1024]{2,1,0:T(8,128)(2,1)}, bf16[3,64,1024]{2,1,0:T(8,128)(2,1)}, u32[]{:S(2)}, u32[]{:S(2)}) collective-permute-start(bf16[3,64,1024]{2,1,0:T(8,128)(2,1)} %collective-permute-done.1.refs_1_), channel_id=1, source_target_pairs={{0,12},{4,0},{8,4},{12,8},{1,13},{5,1},{9,5},{13,9},{2,14},{6,2},{... | collective-permute-start | bytes 1179656 | tf_op jit(solution)/shard_map/ppermute | solution.py:40
  59.7 4.7 %all-to-all-start.1 = ((bf16[4,4,48,1024]{3,2,1,0:T(8,128)(2,1)}), bf16[4,4,48,1024]{3,2,1,0:T(8,128)(2,1)S(1)}, u32[]{:S(2)}, u32[]{:S(2)}) async-start(bf16[4,4,48,1024]{3,2,1,0:T(8,128)(2,1)} %get-tuple-element.76), calls=%async_computation.1 | async-start | bytes 3145728 | tf_op jit(solution)/shard_map/all_to_all | solution.py:48
  64.4 2.1 collective-permute-done.11.refs_5_
  66.5 3.4 %collective-permute-done.9.refs_3_ = bf16[3,64,1024]{2,1,0:T(8,128)(2,1)} collective-permute-done((bf16[3,64,1024]{2,1,0:T(8,128)(2,1)}, bf16[3,64,1024]{2,1,0:T(8,128)(2,1)}, u32[]{:S(2)}, u32[]{:S(2)}) %collective-permute-start.9) | collective-permute-done | bytes 393248 | tf_op jit(solution)/shard_map/ppermute | solution.py:40
  69.9 3.2 %shard_map.123 = (bf16[6,3,64,1024]{3,2,1,0:T(8,128)(2,1)}, bf16[3,64,1024]{2,1,0:T(8,128)(2,1)}, bf16[3,64,1024]{2,1,0:T(8,128)(2,1)}) custom-call(bf16[3,64,1024]{2,1,0:T(8,128)(2,1)S(1)} %broadcast_select_fusion.refs_0_, bf16[3,64,1024]{2,1,0:T(8,128)(2,1)} %collective-permute-done.1.refs_1_, bf16[3,64,1024]{2,1,0:T(8,128)(2,1)} %collective-permute-done.8.refs_2_, ...), custom_call_target="tpu_custom_call" | custom-call | bytes 4194304 | tf_op jit(solution)/shard_map/pallas_call | solution.py:81
  73.1 1.3 shard_map.121
  74.4 2.7 %collective-permute-start.14 = (bf16[3,64,1024]{2,1,0:T(8,128)(2,1)}, bf16[3,64,1024]{2,1,0:T(8,128)(2,1)S(1)}, u32[]{:S(2)}, u32[]{:S(2)}) collective-permute-start(bf16[3,64,1024]{2,1,0:T(8,128)(2,1)} %get-tuple-element.84), channel_id=1, source_target_pairs={{0,12},{4,0},{8,4},{12,8},{1,13},{5,1},{9,5},{13,9},{2,14},{6,2},{... | collective-permute-start | bytes 1179656 | tf_op jit(solution)/shard_map/ppermute | solution.py:40
  77.1 5.3 %all-to-all-done.1.refs_0_ = bf16[4,4,48,1024]{3,2,1,0:T(8,128)(2,1)S(1)} async-done(((bf16[4,4,48,1024]{3,2,1,0:T(8,128)(2,1)}), bf16[4,4,48,1024]{3,2,1,0:T(8,128)(2,1)S(1)}, u32[]{:S(2)}, u32[]{:S(2)}) %all-to-all-start.1) | async-done | bytes 1572896 | tf_op jit(solution)/shard_map/all_to_all | solution.py:48
  82.4 5.2 %all-to-all-start = ((bf16[4,4,48,1024]{3,2,1,0:T(8,128)(2,1)}), bf16[4,4,48,1024]{3,2,1,0:T(8,128)(2,1)}, u32[]{:S(2)}, u32[]{:S(2)}) async-start(bf16[4,4,48,1024]{3,2,1,0:T(8,128)(2,1)} %shard_map.121), calls=%async_computation | async-start | bytes 3145728 | tf_op jit(solution)/shard_map/all_to_all | solution.py:48
  89.6 8.8 %collective-permute-done.5.c1 = bf16[4,48,1024]{2,1,0:T(8,128)(2,1)S(1)} collective-permute-done((bf16[4,48,1024]{2,1,0:T(8,128)(2,1)S(1)}, bf16[4,48,1024]{2,1,0:T(8,128)(2,1)S(1)}, u32[]{:S(2)}, u32[]{:S(2)}) %collective-permute-start.5) | collective-permute-done | bytes 393248 | tf_op jit(solution)/shard_map/ppermute | solution.py:36
  98.4 7.0 %collective-permute-done.6.c2 = bf16[4,48,1024]{2,1,0:T(8,128)(2,1)S(1)} collective-permute-done((bf16[4,48,1024]{2,1,0:T(8,128)(2,1)S(1)}, bf16[4,48,1024]{2,1,0:T(8,128)(2,1)S(1)}, u32[]{:S(2)}, u32[]{:S(2)}) %collective-permute-start.6) | collective-permute-done | bytes 393248 | tf_op jit(solution)/shard_map/ppermute | solution.py:36
  105.4 4.3 %collective-permute-done.7.c3 = bf16[4,48,1024]{2,1,0:T(8,128)(2,1)S(1)} collective-permute-done((bf16[4,48,1024]{2,1,0:T(8,128)(2,1)S(1)}, bf16[4,48,1024]{2,1,0:T(8,128)(2,1)S(1)}, u32[]{:S(2)}, u32[]{:S(2)}) %collective-permute-start.7) | collective-permute-done | bytes 393248 | tf_op jit(solution)/shard_map/ppermute | solution.py:36
  110.7 25.5 %shard_map.125 = (bf16[4,48,1024]{2,1,0:T(8,128)(2,1)S(1)}, bf16[4,48,1024]{2,1,0:T(8,128)(2,1)S(1)}, bf16[4,48,1024]{2,1,0:T(8,128)(2,1)S(1)}, bf16[4,48,1024]{...) custom-call(s32[4]{0:T(128)S(1)} %pad_add_fusion.place, ...), custom_call_target="tpu_custom_call" | custom-call | flops 14495514624 | bytes 20971520 | tf_op jit(solution)/shard_map/pallas_call | solution.py:317
  138.5 5.6 %all-to-all-start.3 = ((bf16[4,4,48,1024]{3,2,1,0:T(8,128)(2,1)}), bf16[4,4,48,1024]{3,2,1,0:T(8,128)(2,1)}, u32[]{:S(2)}, u32[]{:S(2)}) async-start(bf16[4,4,48,1024]{3,2,1,0:T(8,128)(2,1)} %get-tuple-element.101), calls=%async_computation.3 | async-start | bytes 3145728 | tf_op jit(solution)/shard_map/all_to_all | solution.py:48
  144.1 2.2 collective-permute-start.20
  146.8 2.1 shard_map.126
  149.0 2.7 %collective-permute-start.18 = (bf16[3,2,32,1024]{3,2,1,0:T(8,128)(2,1)S(1)}, bf16[3,2,32,1024]{3,2,1,0:T(8,128)(2,1)S(1)}, u32[]{:S(2)}, u32[]{:S(2)}) collective-permute-start(bf16[3,2,32,1024]{3,2,1,0:T(8,128)(2,1)S(1)} %get-tuple-element.88), channel_id=1, source_target_pairs={{0,12},{4,0},{8,4},{12,8},{1,13},{5,1},{9,5},{13,9},{2,14},{6,2},{... | collective-permute-start | bytes 1179656 | tf_op jit(solution)/shard_map/ppermute | solution.py:40
  151.8 3.6 %collective-permute-done.19.refs_1_ = bf16[4,48,1024]{2,1,0:T(8,128)(2,1)S(1)} collective-permute-done((bf16[4,48,1024]{2,1,0:T(8,128)(2,1)}, bf16[4,48,1024]{2,1,0:T(8,128)(2,1)S(1)}, u32[]{:S(2)}, u32[]{:S(2)}) %collective-permute-start.19) | collective-permute-done | bytes 393248 | tf_op jit(solution)/shard_map/ppermute | solution.py:36
  155.4 2.9 %collective-permute-done.20.refs_2_ = bf16[4,48,1024]{2,1,0:T(8,128)(2,1)S(1)} collective-permute-done((bf16[4,48,1024]{2,1,0:T(8,128)(2,1)}, bf16[4,48,1024]{2,1,0:T(8,128)(2,1)S(1)}, u32[]{:S(2)}, u32[]{:S(2)}) %collective-permute-start.20) | collective-permute-done | bytes 393248 | tf_op jit(solution)/shard_map/ppermute | solution.py:36
  158.3 6.4 %collective-permute-done.21.refs_3_ = bf16[4,48,1024]{2,1,0:T(8,128)(2,1)S(1)} collective-permute-done((bf16[4,48,1024]{2,1,0:T(8,128)(2,1)}, bf16[4,48,1024]{2,1,0:T(8,128)(2,1)S(1)}, u32[]{:S(2)}, u32[]{:S(2)}) %collective-permute-start.21) | collective-permute-done | bytes 393248 | tf_op jit(solution)/shard_map/ppermute | solution.py:36
  166.3 1.2 copy-done.1
  167.5 4.9 %all-to-all-start.2 = ((bf16[4,4,48,1024]{3,2,1,0:T(8,128)(2,1)}), bf16[4,4,48,1024]{3,2,1,0:T(8,128)(2,1)}, u32[]{:S(2)}, u32[]{:S(2)}) async-start(bf16[4,4,48,1024]{3,2,1,0:T(8,128)(2,1)} %copy-done.1), calls=%async_computation.2 | async-start | bytes 3145728 | tf_op jit(solution)/shard_map/all_to_all | solution.py:48
  172.4 1.0 copy-done.8
  173.4 2.5 %shard_map.129 = (bf16[3,2,64,1024]{3,2,1,0:T(8,128)(2,1)S(1)}, bf16[3,2,64,1024]{3,2,1,0:T(8,128)(2,1)S(1)}) custom-call(bf16[4,3,2,64,1024]{4,3,2,1,0:T(8,128)(2,1)S(1)} %copy-done, bf16[4,3,2,64,1024]{4,3,2,1,0:T(8,128)(2,1)} %collective-permute-done.16.came, bf16[3,2,32,1024]{3,2,1,0:T(8,128)(2,1)S(1)} %copy-done.6, bf16[3,2,32,1024]{3,2,1,0:T(8,128)(2,1)S(1)} %copy-done.8), custom_call_target="tpu_custom_call" | custom-call | bytes 1048576 | tf_op jit(solution)/shard_map/pallas_call | solution.py:334
  176.0 2.7 %collective-permute-start.23 = (bf16[3,2,64,1024]{3,2,1,0:T(8,128)(2,1)S(1)}, bf16[3,2,64,1024]{3,2,1,0:T(8,128)(2,1)S(1)}, u32[]{:S(2)}, u32[]{:S(2)}) collective-permute-start(bf16[3,2,64,1024]{3,2,1,0:T(8,128)(2,1)S(1)} %get-tuple-element.100), channel_id=1, source_target_pairs={{0,12},{4,0},{8,4},{12,8},{1,13},{5,1},{9,5},{13,9},{2,14},{6,2},{... | collective-permute-start | bytes 2359304 | tf_op jit(solution)/shard_map/ppermute | solution.py:40
  178.7 1.5 shard_map.130
  180.3 3.3 %collective-permute-start.25 = (bf16[4,48,1024]{2,1,0:T(8,128)(2,1)S(1)}, bf16[4,48,1024]{2,1,0:T(8,128)(2,1)S(1)}, u32[]{:S(2)}, u32[]{:S(2)}) collective-permute-start(bf16[4,48,1024]{2,1,0:T(8,128)(2,1)S(1)} %get-tuple-element.104), channel_id=1, source_target_pairs={{32,0},{35,1},{34,2},{33,3},{36,4},{39,5},{38,6},{37,7},{40,8},{43... | collective-permute-start | bytes 1179656 | tf_op jit(solution)/shard_map/ppermute | solution.py:36
  183.6 7.5 %collective-permute-done.24 = bf16[4,48,1024]{2,1,0:T(8,128)(2,1)S(1)} collective-permute-done((bf16[4,48,1024]{2,1,0:T(8,128)(2,1)S(1)}, bf16[4,48,1024]{2,1,0:T(8,128)(2,1)S(1)}, u32[]{:S(2)}, u32[]{:S(2)}) %collective-permute-start.24) | collective-permute-done | bytes 393248 | tf_op jit(solution)/shard_map/ppermute | solution.py:36
  191.2 3.9 %collective-permute-done.25 = bf16[4,48,1024]{2,1,0:T(8,128)(2,1)S(1)} collective-permute-done((bf16[4,48,1024]{2,1,0:T(8,128)(2,1)S(1)}, bf16[4,48,1024]{2,1,0:T(8,128)(2,1)S(1)}, u32[]{:S(2)}, u32[]{:S(2)}) %collective-permute-start.25) | collective-permute-done | bytes 393248 | tf_op jit(solution)/shard_map/ppermute | solution.py:36
  195.0 6.7 %collective-permute-done.26 = bf16[4,48,1024]{2,1,0:T(8,128)(2,1)S(1)} collective-permute-done((bf16[4,48,1024]{2,1,0:T(8,128)(2,1)S(1)}, bf16[4,48,1024]{2,1,0:T(8,128)(2,1)S(1)}, u32[]{:S(2)}, u32[]{:S(2)}) %collective-permute-start.26) | collective-permute-done | bytes 393248 | tf_op jit(solution)/shard_map/ppermute | solution.py:36
  201.7 3.0 %shard_map.132 = (bf16[3,64,1024]{2,1,0:T(8,128)(2,1)}, f32[3,64,1024]{2,1,0:T(8,128)S(1)}) custom-call(s32[4]{0:T(128)S(1)} %pad_add_fusion.place, bf16[4,3,2,64,1024]{4,3,2,1,0:T(8,128)(2,1)S(1)} %copy-done, bf16[4,3,2,64,1024]{4,3,2,1,0:T(8,128)(2,1)} %collective-permute-done.16.came, bf16[3,2,64,1024]{3,2,1,0:T(8,128)(2,1)S(1)} %collective-permute-done.22.fr, ...), custom_call_target="tpu_custom_call" | custom-call | bytes 1048576 | tf_op jit(solution)/shard_map/pallas_call | solution.py:339
  205.6 1.6 collective-permute-start.27
  207.2 1.6 shard_map.131
  208.8 3.3 %shard_map.128 = bf16[256,1024]{1,0:T(8,128)(2,1)} custom-call(s32[256,4]{1,0:T(8,128)S(1)} %copy-done.10, f32[256,2]{1,0:T(8,128)S(1)} %copy-done.12, bf16[768,1024]{1,0:T(8,128)(2,1)} %bitcast.8.rows_ref), custom_call_target="tpu_custom_call" | custom-call | flops 805306368 | bytes 2097152 | tf_op jit(solution)/shard_map/pallas_call | solution.py:343
  212.1 17.0 %collective-permute-done.27.came = bf16[3,64,1024]{2,1,0:T(8,128)(2,1)S(1)} collective-permute-done((bf16[3,64,1024]{2,1,0:T(8,128)(2,1)}, bf16[3,64,1024]{2,1,0:T(8,128)(2,1)S(1)}, u32[]{:S(2)}, u32[]{:S(2)}) %collective-permute-start.27) | collective-permute-done | bytes 393248 | tf_op jit(solution)/shard_map/ppermute | solution.py:52
  (88 shorter events, 14.6 us)
Async XLA Ops:
  0.6 0.9 copy-start.13
  3.4 12.5 %collective-permute-start = (bf16[3,64,1024]{2,1,0:T(8,128)(2,1)S(1)}, bf16[3,64,1024]{2,1,0:T(8,128)(2,1)S(1)}, u32[]{:S(2)}, u32[]{:S(2)}) collective-permute-start(bf16[3,64,1024]{2,1,0:T(8,128)(2,1)S(1)} %shard_map.120), channel_id=1, source_target_pairs={{0,128},{64,192},{128,0},{192,64},{1,129},{65,193},{129,1},{193,65... | collective-permute-start | bytes 1179656 | tf_op jit(solution)/shard_map/ppermute | solution.py:44
  6.1 9.8 %copy-start.11 = (f32[256,2]{1,0:T(8,128)}, f32[256,2]{1,0:T(8,128)S(1)}, u32[]{:S(2)}) copy-start(f32[256,2]{1,0:T(8,128)S(1)} %copy.14.gate_ref) | copy-start | bytes 6148
  10.3 1.0 copy-start.17
  11.4 1.0 copy-start.18
  15.9 41.1 %copy-start.9 = (s32[256,4]{1,0:T(8,128)}, s32[256,4]{1,0:T(8,128)S(1)}, u32[]{:S(2)}) copy-start(s32[256,4]{1,0:T(8,128)S(1)} %get-tuple-element.61.slot_ref) | copy-start | bytes 12292
  16.0 13.2 %collective-permute-start.2 = (bf16[4,48,1024]{2,1,0:T(8,128)(2,1)S(1)}, bf16[4,48,1024]{2,1,0:T(8,128)(2,1)S(1)}, u32[]{:S(2)}, u32[]{:S(2)}) collective-permute-start(bf16[4,48,1024]{2,1,0:T(8,128)(2,1)S(1)} %get-tuple-element.69), channel_id=1, source_target_pairs={{0,16},{1,17},{2,18},{3,19},{4,20},{5,21},{6,22},{7,23},{8,24},{9,... | collective-permute-start | bytes 1179656 | tf_op jit(solution)/shard_map/ppermute | solution.py:36
  18.9 14.7 %collective-permute-start.3 = (bf16[4,48,1024]{2,1,0:T(8,128)(2,1)S(1)}, bf16[4,48,1024]{2,1,0:T(8,128)(2,1)S(1)}, u32[]{:S(2)}, u32[]{:S(2)}) collective-permute-start(bf16[4,48,1024]{2,1,0:T(8,128)(2,1)S(1)} %get-tuple-element.70), channel_id=1, source_target_pairs={{0,32},{1,35},{2,34},{3,33},{4,36},{5,39},{6,38},{7,37},{8,40},{9,... | collective-permute-start | bytes 1179656 | tf_op jit(solution)/shard_map/ppermute | solution.py:36
  18.9 21.7 %collective-permute-start.4 = (bf16[4,48,1024]{2,1,0:T(8,128)(2,1)S(1)}, bf16[4,48,1024]{2,1,0:T(8,128)(2,1)S(1)}, u32[]{:S(2)}, u32[]{:S(2)}) collective-permute-start(bf16[4,48,1024]{2,1,0:T(8,128)(2,1)S(1)} %get-tuple-element.71), channel_id=1, source_target_pairs={{0,50},{1,51},{2,48},{3,49},{4,54},{5,55},{6,52},{7,53},{8,58},{9,... | collective-permute-start | bytes 1179656 | tf_op jit(solution)/shard_map/ppermute | solution.py:36
  18.9 38.1 %collective-permute-start.1 = (bf16[3,64,1024]{2,1,0:T(8,128)(2,1)S(1)}, bf16[3,64,1024]{2,1,0:T(8,128)(2,1)}, u32[]{:S(2)}, u32[]{:S(2)}) collective-permute-start(bf16[3,64,1024]{2,1,0:T(8,128)(2,1)S(1)} %broadcast_select_fusion.refs_0_), channel_id=1, source_target_pairs={{0,2},{2,0},{1,3},{3,1},{4,6},{6,4},{5,7},{7,5},{8,10},{10,8},{9,1... | collective-permute-start | bytes 1179656 | tf_op jit(solution)/shard_map/ppermute | solution.py:52
  22.9 41.5 %collective-permute-start.10 = (bf16[3,64,1024]{2,1,0:T(8,128)(2,1)S(1)}, bf16[3,64,1024]{2,1,0:T(8,128)(2,1)}, u32[]{:S(2)}, u32[]{:S(2)}) collective-permute-start(bf16[3,64,1024]{2,1,0:T(8,128)(2,1)S(1)} %broadcast_select_fusion.refs_0_), channel_id=1, source_target_pairs={{0,12},{4,0},{8,4},{12,8},{1,13},{5,1},{9,5},{13,9},{2,14},{6,2},{... | collective-permute-start | bytes 1179656 | tf_op jit(solution)/shard_map/ppermute | solution.py:40
  29.1 35.3 %collective-permute-start.8 = (bf16[3,64,1024]{2,1,0:T(8,128)(2,1)S(1)}, bf16[3,64,1024]{2,1,0:T(8,128)(2,1)}, u32[]{:S(2)}, u32[]{:S(2)}) collective-permute-start(bf16[3,64,1024]{2,1,0:T(8,128)(2,1)S(1)} %broadcast_select_fusion.refs_0_), channel_id=1, source_target_pairs={{0,4},{4,8},{8,12},{12,0},{1,5},{5,9},{9,13},{13,1},{2,6},{6,10},{... | collective-permute-start | bytes 1179656 | tf_op jit(solution)/shard_map/ppermute | solution.py:40
  57.0 9.5 %collective-permute-start.11 = (bf16[3,64,1024]{2,1,0:T(8,128)(2,1)}, bf16[3,64,1024]{2,1,0:T(8,128)(2,1)}, u32[]{:S(2)}, u32[]{:S(2)}) collective-permute-start(bf16[3,64,1024]{2,1,0:T(8,128)(2,1)} %collective-permute-done.1.refs_1_), channel_id=1, source_target_pairs={{0,12},{4,0},{8,4},{12,8},{1,13},{5,1},{9,5},{13,9},{2,14},{6,2},{... | collective-permute-start | bytes 1179656 | tf_op jit(solution)/shard_map/ppermute | solution.py:40
  59.7 10.2 %collective-permute-start.9 = (bf16[3,64,1024]{2,1,0:T(8,128)(2,1)}, bf16[3,64,1024]{2,1,0:T(8,128)(2,1)}, u32[]{:S(2)}, u32[]{:S(2)}) collective-permute-start(bf16[3,64,1024]{2,1,0:T(8,128)(2,1)} %collective-permute-done.1.refs_1_), channel_id=1, source_target_pairs={{0,4},{4,8},{8,12},{12,0},{1,5},{5,9},{9,13},{13,1},{2,6},{6,10},{... | collective-permute-start | bytes 1179656 | tf_op jit(solution)/shard_map/ppermute | solution.py:40
  59.7 22.7 %all-to-all-start.1 = ((bf16[4,4,48,1024]{3,2,1,0:T(8,128)(2,1)}), bf16[4,4,48,1024]{3,2,1,0:T(8,128)(2,1)S(1)}, u32[]{:S(2)}, u32[]{:S(2)}) async-start(bf16[4,4,48,1024]{3,2,1,0:T(8,128)(2,1)} %get-tuple-element.76), calls=%async_computation.1 | async-start | bytes 3145728 | tf_op jit(solution)/shard_map/all_to_all | solution.py:48
  73.1 36.6 %collective-permute-start.12 = (bf16[6,3,64,1024]{3,2,1,0:T(8,128)(2,1)}, bf16[6,3,64,1024]{3,2,1,0:T(8,128)(2,1)}, u32[]{:S(2)}, u32[]{:S(2)}) collective-permute-start(bf16[6,3,64,1024]{3,2,1,0:T(8,128)(2,1)} %get-tuple-element.82.near), channel_id=1, source_target_pairs={{0,1},{1,0},{2,3},{3,2},{4,5},{5,4},{6,7},{7,6},{8,9},{9,8},{10,11... | collective-permute-start | bytes 7077896 | tf_op jit(solution)/shard_map/ppermute | solution.py:52
  74.4 13.2 %collective-permute-start.13 = (bf16[3,64,1024]{2,1,0:T(8,128)(2,1)}, bf16[3,64,1024]{2,1,0:T(8,128)(2,1)S(1)}, u32[]{:S(2)}, u32[]{:S(2)}) collective-permute-start(bf16[3,64,1024]{2,1,0:T(8,128)(2,1)} %get-tuple-element.83), channel_id=1, source_target_pairs={{0,4},{4,8},{8,12},{12,0},{1,5},{5,9},{9,13},{13,1},{2,6},{6,10},{... | collective-permute-start | bytes 1179656 | tf_op jit(solution)/shard_map/ppermute | solution.py:40
  74.4 13.2 %collective-permute-start.14 = (bf16[3,64,1024]{2,1,0:T(8,128)(2,1)}, bf16[3,64,1024]{2,1,0:T(8,128)(2,1)S(1)}, u32[]{:S(2)}, u32[]{:S(2)}) collective-permute-start(bf16[3,64,1024]{2,1,0:T(8,128)(2,1)} %get-tuple-element.84), channel_id=1, source_target_pairs={{0,12},{4,0},{8,4},{12,8},{1,13},{5,1},{9,5},{13,9},{2,14},{6,2},{... | collective-permute-start | bytes 1179656 | tf_op jit(solution)/shard_map/ppermute | solution.py:40
  82.4 27.3 %all-to-all-start = ((bf16[4,4,48,1024]{3,2,1,0:T(8,128)(2,1)}), bf16[4,4,48,1024]{3,2,1,0:T(8,128)(2,1)}, u32[]{:S(2)}, u32[]{:S(2)}) async-start(bf16[4,4,48,1024]{3,2,1,0:T(8,128)(2,1)} %shard_map.121), calls=%async_computation | async-start | bytes 3145728 | tf_op jit(solution)/shard_map/all_to_all | solution.py:48
  87.6 23.1 %copy-start.2 = (bf16[2,3,64,1024]{3,2,1,0:T(8,128)(2,1)}, bf16[2,3,64,1024]{3,2,1,0:T(8,128)(2,1)S(1)}, u32[]{:S(2)}) copy-start(bf16[2,3,64,1024]{3,2,1,0:T(8,128)(2,1)S(1)} %shard_map.124.far) | copy-start | bytes 2359300
  87.6 22.1 %collective-permute-start.15 = (bf16[2,3,64,1024]{3,2,1,0:T(8,128)(2,1)S(1)}, bf16[2,3,64,1024]{3,2,1,0:T(8,128)(2,1)S(1)}, u32[]{:S(2)}, u32[]{:S(2)}) collective-permute-start(bf16[2,3,64,1024]{3,2,1,0:T(8,128)(2,1)S(1)} %shard_map.124.far), channel_id=1, source_target_pairs={{0,1},{1,0},{2,3},{3,2},{4,5},{5,4},{6,7},{7,6},{8,9},{9,8},{10,11... | collective-permute-start | bytes 2359304 | tf_op jit(solution)/shard_map/ppermute | solution.py:52
  87.9 10.6 %collective-permute-start.5 = (bf16[4,48,1024]{2,1,0:T(8,128)(2,1)S(1)}, bf16[4,48,1024]{2,1,0:T(8,128)(2,1)S(1)}, u32[]{:S(2)}, u32[]{:S(2)}) collective-permute-start(bf16[4,48,1024]{2,1,0:T(8,128)(2,1)S(1)} %get-tuple-element.78), channel_id=1, source_target_pairs={{0,16},{1,17},{2,18},{3,19},{4,20},{5,21},{6,22},{7,23},{8,24},{9,... | collective-permute-start | bytes 1179656 | tf_op jit(solution)/shard_map/ppermute | solution.py:36
  88.1 17.2 %collective-permute-start.6 = (bf16[4,48,1024]{2,1,0:T(8,128)(2,1)S(1)}, bf16[4,48,1024]{2,1,0:T(8,128)(2,1)S(1)}, u32[]{:S(2)}, u32[]{:S(2)}) collective-permute-start(bf16[4,48,1024]{2,1,0:T(8,128)(2,1)S(1)} %get-tuple-element.79), channel_id=1, source_target_pairs={{0,32},{1,35},{2,34},{3,33},{4,36},{5,39},{6,38},{7,37},{8,40},{9,... | collective-permute-start | bytes 1179656 | tf_op jit(solution)/shard_map/ppermute | solution.py:36
  88.7 21.0 %collective-permute-start.7 = (bf16[4,48,1024]{2,1,0:T(8,128)(2,1)S(1)}, bf16[4,48,1024]{2,1,0:T(8,128)(2,1)S(1)}, u32[]{:S(2)}, u32[]{:S(2)}) collective-permute-start(bf16[4,48,1024]{2,1,0:T(8,128)(2,1)S(1)} %get-tuple-element.80), channel_id=1, source_target_pairs={{0,50},{1,51},{2,48},{3,49},{4,54},{5,55},{6,52},{7,53},{8,58},{9,... | collective-permute-start | bytes 1179656 | tf_op jit(solution)/shard_map/ppermute | solution.py:36
  98.4 12.3 %copy-start.23 = (bf16[4,48,1024]{2,1,0:T(8,128)(2,1)}, bf16[4,48,1024]{2,1,0:T(8,128)(2,1)S(1)}, u32[]{:S(2)}) copy-start(bf16[4,48,1024]{2,1,0:T(8,128)(2,1)S(1)} %collective-permute-done.5.c1) | copy-start | bytes 1179652
  105.4 4.4 %copy-start.24 = (bf16[4,48,1024]{2,1,0:T(8,128)(2,1)}, bf16[4,48,1024]{2,1,0:T(8,128)(2,1)S(1)}, u32[]{:S(2)}) copy-start(bf16[4,48,1024]{2,1,0:T(8,128)(2,1)S(1)} %collective-permute-done.6.c2) | copy-start | bytes 1179652
  109.7 1.0 copy-start.22
  138.5 8.3 %collective-permute-start.16 = (bf16[4,3,2,64,1024]{4,3,2,1,0:T(8,128)(2,1)}, bf16[4,3,2,64,1024]{4,3,2,1,0:T(8,128)(2,1)}, u32[]{:S(2)}, u32[]{:S(2)}) collective-permute-start(bf16[4,3,2,64,1024]{4,3,2,1,0:T(8,128)(2,1)} %get-tuple-element.86), channel_id=1, source_target_pairs={{0,1},{1,0},{2,3},{3,2},{4,5},{5,4},{6,7},{7,6},{8,9},{9,8},{10,11... | collective-permute-start | bytes 9437192 | tf_op jit(solution)/shard_map/ppermute | solution.py:52
  138.5 8.3 %copy-start = (bf16[4,3,2,64,1024]{4,3,2,1,0:T(8,128)(2,1)S(1)}, bf16[4,3,2,64,1024]{4,3,2,1,0:T(8,128)(2,1)}, u32[]{:S(2)}) copy-start(bf16[4,3,2,64,1024]{4,3,2,1,0:T(8,128)(2,1)} %get-tuple-element.85.mine) | copy-start | bytes 9437188
  138.5 29.0 %all-to-all-start.3 = ((bf16[4,4,48,1024]{3,2,1,0:T(8,128)(2,1)}), bf16[4,4,48,1024]{3,2,1,0:T(8,128)(2,1)}, u32[]{:S(2)}, u32[]{:S(2)}) async-start(bf16[4,4,48,1024]{3,2,1,0:T(8,128)(2,1)} %get-tuple-element.101), calls=%async_computation.3 | async-start | bytes 3145728 | tf_op jit(solution)/shard_map/all_to_all | solution.py:48
  144.1 11.3 %collective-permute-start.19 = (bf16[4,48,1024]{2,1,0:T(8,128)(2,1)}, bf16[4,48,1024]{2,1,0:T(8,128)(2,1)S(1)}, u32[]{:S(2)}, u32[]{:S(2)}) collective-permute-start(bf16[4,48,1024]{2,1,0:T(8,128)(2,1)} %copy-done.21), channel_id=1, source_target_pairs={{16,0},{17,1},{18,2},{19,3},{20,4},{21,5},{22,6},{23,7},{24,8},{25... | collective-permute-start | bytes 1179656 | tf_op jit(solution)/shard_map/ppermute | solution.py:36
  144.1 14.2 %collective-permute-start.20 = (bf16[4,48,1024]{2,1,0:T(8,128)(2,1)}, bf16[4,48,1024]{2,1,0:T(8,128)(2,1)S(1)}, u32[]{:S(2)}, u32[]{:S(2)}) collective-permute-start(bf16[4,48,1024]{2,1,0:T(8,128)(2,1)} %copy-done.20), channel_id=1, source_target_pairs={{32,0},{35,1},{34,2},{33,3},{36,4},{39,5},{38,6},{37,7},{40,8},{43... | collective-permute-start | bytes 1179656 | tf_op jit(solution)/shard_map/ppermute | solution.py:36
  146.3 18.4 %collective-permute-start.21 = (bf16[4,48,1024]{2,1,0:T(8,128)(2,1)}, bf16[4,48,1024]{2,1,0:T(8,128)(2,1)S(1)}, u32[]{:S(2)}, u32[]{:S(2)}) collective-permute-start(bf16[4,48,1024]{2,1,0:T(8,128)(2,1)} %copy-done.19), channel_id=1, source_target_pairs={{50,0},{51,1},{48,2},{49,3},{54,4},{55,5},{52,6},{53,7},{58,8},{59... | collective-permute-start | bytes 1179656 | tf_op jit(solution)/shard_map/ppermute | solution.py:36
  148.9 15.8 %collective-permute-start.17 = (bf16[3,2,32,1024]{3,2,1,0:T(8,128)(2,1)S(1)}, bf16[3,2,32,1024]{3,2,1,0:T(8,128)(2,1)S(1)}, u32[]{:S(2)}, u32[]{:S(2)}) collective-permute-start(bf16[3,2,32,1024]{3,2,1,0:T(8,128)(2,1)S(1)} %get-tuple-element.87), channel_id=1, source_target_pairs={{0,4},{4,8},{8,12},{12,0},{1,5},{5,9},{9,13},{13,1},{2,6},{6,10},{... | collective-permute-start | bytes 1179656 | tf_op jit(solution)/shard_map/ppermute | solution.py:40
  149.0 16.4 %collective-permute-start.18 = (bf16[3,2,32,1024]{3,2,1,0:T(8,128)(2,1)S(1)}, bf16[3,2,32,1024]{3,2,1,0:T(8,128)(2,1)S(1)}, u32[]{:S(2)}, u32[]{:S(2)}) collective-permute-start(bf16[3,2,32,1024]{3,2,1,0:T(8,128)(2,1)S(1)} %get-tuple-element.88), channel_id=1, source_target_pairs={{0,12},{4,0},{8,4},{12,8},{1,13},{5,1},{9,5},{13,9},{2,14},{6,2},{... | collective-permute-start | bytes 1179656 | tf_op jit(solution)/shard_map/ppermute | solution.py:40
  166.3 1.2 copy-start.1
  167.5 4.9 %copy-start.6 = (bf16[3,2,32,1024]{3,2,1,0:T(8,128)(2,1)S(1)}, bf16[3,2,32,1024]{3,2,1,0:T(8,128)(2,1)}, u32[]{:S(2)}) copy-start(bf16[3,2,32,1024]{3,2,1,0:T(8,128)(2,1)} %copy-done.5) | copy-start | bytes 1179652
  167.5 41.3 %all-to-all-start.2 = ((bf16[4,4,48,1024]{3,2,1,0:T(8,128)(2,1)}), bf16[4,4,48,1024]{3,2,1,0:T(8,128)(2,1)}, u32[]{:S(2)}, u32[]{:S(2)}) async-start(bf16[4,4,48,1024]{3,2,1,0:T(8,128)(2,1)} %copy-done.1), calls=%async_computation.2 | async-start | bytes 3145728 | tf_op jit(solution)/shard_map/all_to_all | solution.py:48
  172.4 1.0 copy-start.8
  175.9 25.8 %collective-permute-start.22 = (bf16[3,2,64,1024]{3,2,1,0:T(8,128)(2,1)S(1)}, bf16[3,2,64,1024]{3,2,1,0:T(8,128)(2,1)S(1)}, u32[]{:S(2)}, u32[]{:S(2)}) collective-permute-start(bf16[3,2,64,1024]{3,2,1,0:T(8,128)(2,1)S(1)} %get-tuple-element.99), channel_id=1, source_target_pairs={{0,4},{4,8},{8,12},{12,0},{1,5},{5,9},{9,13},{13,1},{2,6},{6,10},{... | collective-permute-start | bytes 2359304 | tf_op jit(solution)/shard_map/ppermute | solution.py:40
  176.0 25.7 %collective-permute-start.23 = (bf16[3,2,64,1024]{3,2,1,0:T(8,128)(2,1)S(1)}, bf16[3,2,64,1024]{3,2,1,0:T(8,128)(2,1)S(1)}, u32[]{:S(2)}, u32[]{:S(2)}) collective-permute-start(bf16[3,2,64,1024]{3,2,1,0:T(8,128)(2,1)S(1)} %get-tuple-element.100), channel_id=1, source_target_pairs={{0,12},{4,0},{8,4},{12,8},{1,13},{5,1},{9,5},{13,9},{2,14},{6,2},{... | collective-permute-start | bytes 2359304 | tf_op jit(solution)/shard_map/ppermute | solution.py:40
  180.2 10.9 %collective-permute-start.24 = (bf16[4,48,1024]{2,1,0:T(8,128)(2,1)S(1)}, bf16[4,48,1024]{2,1,0:T(8,128)(2,1)S(1)}, u32[]{:S(2)}, u32[]{:S(2)}) collective-permute-start(bf16[4,48,1024]{2,1,0:T(8,128)(2,1)S(1)} %get-tuple-element.103), channel_id=1, source_target_pairs={{16,0},{17,1},{18,2},{19,3},{20,4},{21,5},{22,6},{23,7},{24,8},{25... | collective-permute-start | bytes 1179656 | tf_op jit(solution)/shard_map/ppermute | solution.py:36
  180.3 14.7 %collective-permute-start.25 = (bf16[4,48,1024]{2,1,0:T(8,128)(2,1)S(1)}, bf16[4,48,1024]{2,1,0:T(8,128)(2,1)S(1)}, u32[]{:S(2)}, u32[]{:S(2)}) collective-permute-start(bf16[4,48,1024]{2,1,0:T(8,128)(2,1)S(1)} %get-tuple-element.104), channel_id=1, source_target_pairs={{32,0},{35,1},{34,2},{33,3},{36,4},{39,5},{38,6},{37,7},{40,8},{43... | collective-permute-start | bytes 1179656 | tf_op jit(solution)/shard_map/ppermute | solution.py:36
  183.6 18.1 %collective-permute-start.26 = (bf16[4,48,1024]{2,1,0:T(8,128)(2,1)S(1)}, bf16[4,48,1024]{2,1,0:T(8,128)(2,1)S(1)}, u32[]{:S(2)}, u32[]{:S(2)}) collective-permute-start(bf16[4,48,1024]{2,1,0:T(8,128)(2,1)S(1)} %get-tuple-element.105), channel_id=1, source_target_pairs={{50,0},{51,1},{48,2},{49,3},{54,4},{55,5},{52,6},{53,7},{58,8},{59... | collective-permute-start | bytes 1179656 | tf_op jit(solution)/shard_map/ppermute | solution.py:36
  201.7 5.5 %copy-start.10 = (s32[256,4]{1,0:T(8,128)S(1)}, s32[256,4]{1,0:T(8,128)}, u32[]{:S(2)}) copy-start(s32[256,4]{1,0:T(8,128)} %copy-done.9) | copy-start | bytes 12292
  205.6 3.2 %copy-start.12 = (f32[256,2]{1,0:T(8,128)S(1)}, f32[256,2]{1,0:T(8,128)}, u32[]{:S(2)}) copy-start(f32[256,2]{1,0:T(8,128)} %copy-done.11) | copy-start | bytes 6148
  205.6 23.5 %collective-permute-start.27 = (bf16[3,64,1024]{2,1,0:T(8,128)(2,1)}, bf16[3,64,1024]{2,1,0:T(8,128)(2,1)S(1)}, u32[]{:S(2)}, u32[]{:S(2)}) collective-permute-start(bf16[3,64,1024]{2,1,0:T(8,128)(2,1)} %get-tuple-element.113), channel_id=1, source_target_pairs={{0,2},{2,0},{1,3},{3,1},{4,6},{6,4},{5,7},{7,5},{8,10},{10,8},{9,1... | collective-permute-start | bytes 1179656 | tf_op jit(solution)/shard_map/ppermute | solution.py:52
  208.8 20.4 %copy-start.4 = (f32[3,64,1024]{2,1,0:T(8,128)S(1)}, f32[3,64,1024]{2,1,0:T(8,128)}, u32[]{:S(2)}) copy-start(f32[3,64,1024]{2,1,0:T(8,128)} %copy-done.3) | copy-start | bytes 2359300
  (10 other events, 7.8 us)
